TPU v7x, 512 devices: a whole 4x4x16 slice. The times are simulated.
512 devices in a mesh: section: 8 (over z_lo), seq: 8 (over z_hi, x), tensor: 8 (over y, core).
Axes of the slice: x: 4, y: 4, z: 16 (z_hi: 2, z_lo: 8; z = z_hi * 8 + z_lo), core: 2. Of those that a mesh axis runs over, the one named last changes fastest.
Arguments:
- acts: bfloat16 [8, 512, 8192], P('section', 'seq', 'tensor'), may hold values from -6 to 6
- incoming: bfloat16 [8, 512, 8192], P('section', 'seq', 'tensor'), may hold values from -6 to 6
- rotation: bfloat16 [8192, 8192], P('tensor', 'seq'), may hold values from -0.0625 to 0.0625
- q_weight: bfloat16 [8, 8192, 8192], P('section', 'seq', 'tensor'), may hold values from -0.0625 to 0.0625
- w_exponents: int32 [8, 8192], P('section', 'tensor'), may hold values from -13 to -9
Outputs:
- r1_grad: float32 [8192, 8192], P(('tensor', 'section'), 'seq')
- grad_rotated: bfloat16 [8, 512, 8192], P('section', 'tensor', 'seq')
All inputs are finite; a program needn't handle non-finite values.
Results may differ from a plain program's by a relative error of at most 0.027.
Values may be sent and summed in bfloat16 or wider, within the bound.
A program may use at most 64 MiB of HBM per device.

v0:
```python
import jax
import jax.numpy as jnp
from jax import lax
from jax.sharding import PartitionSpec as P

act_clip = 0.5


def shifted_2(block, axis, distance):
    devices = range(lax.axis_size(axis))
    route = [(i - distance, i) for i in devices if i - distance in devices]
    return lax.ppermute(block, axis, route)


def body(acts, incoming, rotation, q_weight, w_exponents):
    section_count = lax.axis_size("section")
    shifted = shifted_2(incoming, "section", -1)
    upstream = jnp.where(lax.axis_index("section") == section_count - 1, incoming, shifted)[0]
    tok_all = lax.all_gather(acts[0], "seq", axis=0, tiled=True)
    block = tok_all
    rotated = lax.psum_scatter(
        jnp.dot(block, rotation, preferred_element_type=jnp.float32).astype(jnp.bfloat16),
        "tensor",
        scatter_dimension=0,
        tiled=True,
    ).astype(jnp.float32)
    peaks = lax.pmax(jnp.max(jnp.abs(rotated), axis=1), "seq")
    clip = act_clip * (peaks + 1e-06)
    scale = 127.0 * jnp.exp2(w_exponents[0].astype(jnp.float32))
    quantized = (
        scale[None, :] * jnp.tanh(q_weight[0].astype(jnp.float32) / scale[None, :])
    ).astype(jnp.bfloat16)
    grad_all = lax.all_gather(upstream, "seq", axis=0, tiled=True)
    block = grad_all
    back = lax.psum_scatter(
        lax.dot_general(
            block, quantized, (((1,), (1,)), ((), ())), preferred_element_type=jnp.float32
        ).astype(jnp.bfloat16),
        "tensor",
        scatter_dimension=0,
        tiled=True,
    ).astype(jnp.float32)
    ratio = jnp.tanh(rotated / clip[:, None])
    grad_rot = (back * (1.0 - ratio * ratio)).astype(jnp.bfloat16)
    block_grad = lax.dot_general(
        tok_all,
        lax.all_gather(grad_rot, "tensor", axis=0, tiled=True),
        (((0,), (0,)), ((), ())),
        preferred_element_type=jnp.float32,
    )
    total = lax.psum_scatter(
        block_grad.astype(jnp.bfloat16), "section", scatter_dimension=0, tiled=True
    ).astype(jnp.float32)
    return (total, grad_rot[None])


def solution(mesh):
    placed = (
        P("section", "seq", "tensor"),
        P("section", "seq", "tensor"),
        P("tensor", "seq"),
        P("section", "seq", "tensor"),
        P("section", "tensor"),
    )
    return jax.shard_map(
        body,
        mesh=mesh,
        in_specs=placed,
        out_specs=(P(("tensor", "section"), "seq"), P("section", "tensor", "seq")),
        check_vma=False,
    )
```

profile of v0, /device:TPU:6, one launch (start us, length us, event | category | flops | bytes accessed | tf_op | source)
XLA Modules:
  0.0 389.1 jit_solution(8738975020512197853)
XLA Ops:
  7.2 0.7 all-gather.10.cloned.1.call-update
  7.9 0.0 all-gather.8.cloned.1.call-start
  8.0 1.3 collective-permute-start
  9.3 6.2 %collective-permute-done = bf16[1,64,1024]{2,1,0:T(8,128)(2,1)S(1)} collective-permute-done((bf16[1,64,1024]{2,1,0:T(8,128)(2,1)}, bf16[1,64,1024]{2,1,0:T(8,128)(2,1)S(1)}, u32[]{:S(2)}, u32[]{:S(2)}) %collective-permute-start) | collective-permute-done | bytes 131104 | tf_op jit(solution)/shard_map/ppermute | solution.py:12
  15.5 0.7 broadcast_select_fusion
  16.2 0.0 reduce-scatter.8.cloned.1.call-start
  16.2 90.2 %all-gather.10.cloned.1.call-done = bf16[1,512,1024]{2,1,0:T(8,128)(2,1)} async-done(((bf16[1,64,1024]{2,1,0:T(8,128)(2,1)}), bf16[1,512,1024]{2,1,0:T(8,128)(2,1)}) %all-gather.10.cloned.1.call-update) | async-done | bytes 1048592 | tf_op jit(solution)/shard_map/all_gather | solution.py:19
  106.5 3.5 convolution_convert_fusion
  110.0 0.0 reduce-scatter.6.cloned.1.call-start
  110.1 82.1 %all-gather.8.cloned.1.call-done = bf16[1,512,1024]{2,1,0:T(8,128)(2,1)} async-done(((bf16[1,64,1024]{2,1,0:T(8,128)(2,1)}), bf16[1,512,1024]{2,1,0:T(8,128)(2,1)}) %all-gather.8.cloned.1.call-update) | async-done | bytes 1048592 | tf_op jit(solution)/shard_map/all_gather | solution.py:33
  192.2 4.3 %fusion.5 = bf16[512,1024]{1,0:T(8,128)(2,1)} fusion(bf16[1,1024,1024]{2,1,0:T(8,128)(2,1)} %param.8, f32[1024]{0:T(1024)S(1)} %bitcast.22, bf16[1,512,1024]{2,1,0:T(8,128)(2,1)} %all-gather.8.cloned.1.call-done), kind=kOutput, calls=%fused_computation.6 | convolution fusion | flops 1078460416 | bytes 4198400 | tf_op jit(solution)/shard_map/dot_general | solution.py:36
  196.5 0.0 all-gather.6.cloned.1.call-start
  196.5 29.1 %reduce-scatter.8.cloned.1.call-done = bf16[64,1024]{1,0:T(8,128)(2,1)} async-done(((bf16[512,1024]{1,0:T(8,128)(2,1)}), bf16[64,1024]{1,0:T(8,128)(2,1)}) %reduce-scatter.8.cloned.1.call-update) | async-done | bytes 131088 | tf_op jit(solution)/shard_map/reduce_scatter | solution.py:21
  225.7 1.0 fusion.11
  226.7 33.4 %pmax.7 = f32[64]{0:T(128)S(1)} all-reduce(f32[64]{0:T(128)S(1)} %fusion.11), channel_id=1, replica_groups=mesh['section'=8,'seq'=8,'tensor'=8] {'seq'}, use_global_device_ids=true, to_apply=%region_3.4 | all-reduce | flops 64 | bytes 512 | tf_op jit(solution)/shard_map/pmax | solution.py:27
  260.1 7.0 %reduce-scatter.6.cloned.1.call-done = bf16[64,1024]{1,0:T(8,128)(2,1)} async-done(((bf16[512,1024]{1,0:T(8,128)(2,1)}), bf16[64,1024]{1,0:T(8,128)(2,1)}) %reduce-scatter.6.cloned.1.call-update) | async-done | bytes 131088 | tf_op jit(solution)/shard_map/reduce_scatter | solution.py:35
  267.1 1.8 fusion.16
  268.9 0.0 reduce-scatter.10.cloned.1.call-start
  268.9 30.4 %all-gather.6.cloned.1.call-done = bf16[512,1024]{1,0:T(8,128)(2,1)} async-done(((bf16[64,1024]{1,0:T(8,128)(2,1)}), bf16[512,1024]{1,0:T(8,128)(2,1)}) %all-gather.6.cloned.1.call-update) | async-done | bytes 1048592 | tf_op jit(solution)/shard_map/all_gather | solution.py:47
  299.3 3.9 convert_bitcast_fusion
  303.2 3.9 %copy.9 = bf16[1024,1024]{1,0:T(8,128)(2,1)} copy(bf16[1024,1024]{0,1:T(8,128)(2,1)} %convert_bitcast_fusion) | data formatting | bytes 4194304
  307.1 73.1 %reduce-scatter.10.cloned.1.call-done = bf16[128,1024]{1,0:T(8,128)(2,1)} async-done(((bf16[1024,1024]{1,0:T(8,128)(2,1)}), bf16[128,1024]{1,0:T(8,128)(2,1)}) %reduce-scatter.10.cloned.1.call-update) | async-done | bytes 262160
  380.2 1.1 copy.10
  381.4 0.9 copy.8
  (14 shorter events, 0.2 us)
Async XLA Ops:
  7.2 99.3 %copy-start = (bf16[1024,1024]{1,0:T(8,128)(2,1)S(1)}, bf16[1024,1024]{1,0:T(8,128)(2,1)}, u32[]{:S(2)}) copy-start(bf16[1024,1024]{1,0:T(8,128)(2,1)} %param.7) | copy-start | bytes 6291460
  7.2 99.3 %all-gather.10.cloned.1.call-start = ((), (), s32[]{:S(2)}) async-start(), calls=%async_computation.7 | async-start | bytes 1179648 | tf_op jit(solution)/shard_map/all_gather | solution.py:19
  7.9 184.3 %all-gather.8.cloned.1.call-start = ((), (), s32[]{:S(2)}) async-start(), calls=%async_computation.6 | async-start | bytes 1179648 | tf_op jit(solution)/shard_map/all_gather | solution.py:33
  8.0 7.5 %collective-permute-start = (bf16[1,64,1024]{2,1,0:T(8,128)(2,1)}, bf16[1,64,1024]{2,1,0:T(8,128)(2,1)S(1)}, u32[]{:S(2)}, u32[]{:S(2)}) collective-permute-start(bf16[1,64,1024]{2,1,0:T(8,128)(2,1)} %param.6), channel_id=1, source_target_pairs={{64,0},{128,64},{192,128},{256,192},{320,256},{384,320},{448,384},... | collective-permute-start | bytes 393224 | tf_op jit(solution)/shard_map/ppermute | solution.py:12
  16.2 93.9 %copy-start.1 = (s32[1,1024]{1,0:T(1,128)S(1)}, s32[1,1024]{1,0:T(1,128)}, u32[]{:S(2)}) copy-start(s32[1,1024]{1,0:T(1,128)} %param.9) | copy-start | bytes 12292
  16.2 209.5 %reduce-scatter.8.cloned.1.call-start = ((), (), s32[]{:S(2)}) async-start(), calls=%async_computation.4 | async-start | bytes 1179648 | tf_op jit(solution)/shard_map/reduce_scatter | solution.py:21
  110.0 157.1 %reduce-scatter.6.cloned.1.call-start = ((), (), s32[]{:S(2)}) async-start(), calls=%async_computation.3 | async-start | bytes 1179648 | tf_op jit(solution)/shard_map/reduce_scatter | solution.py:35
  192.2 107.2 %copy-start.2 = (bf16[1,512,1024]{2,1,0:T(8,128)(2,1)S(1)}, bf16[1,512,1024]{2,1,0:T(8,128)(2,1)}, u32[]{:S(2)}) copy-start(bf16[1,512,1024]{2,1,0:T(8,128)(2,1)} %all-gather.10.cloned.1.call-done) | copy-start | bytes 3145732
  196.5 102.8 %all-gather.6.cloned.1.call-start = ((), (), s32[]{:S(2)}) async-start(), calls=%async_computation.5 | async-start | bytes 1179648 | tf_op jit(solution)/shard_map/all_gather | solution.py:47
  268.9 111.4 %reduce-scatter.10.cloned.1.call-start = ((), (), s32[]{:S(2)}) async-start(), calls=%async_computation.8 | async-start | bytes 2359296
Sparse Core Ops, SparseCore 0:
  11.2 95.2 all-gather.9
  110.3 81.8 all-gather.7
  195.0 30.6 reduce-scatter.7
  228.3 38.6 reduce-scatter.5
  269.6 29.6 all-gather.5
  307.3 72.9 reduce-scatter.9
where the time goes:
time: 389 us
  waiting for transfers between devices  319 us (82%)
  blocking collectives  33.4 us (9%)
  between operations  14.2 us (4%)
  matrix products  11.7 us (3%)
  local copies, waits for them, and re-layouts  6 us (2%)
    all_gather x1, waiting for transfers between devices, body(): tok_all = lax.all_gather(acts[0], 'seq', axis=0, tiled=True)  90.2 us
    all_gather x1, waiting for transfers between devices, body(): grad_all = lax.all_gather(upstream, 'seq', axis=0, tiled=True)  82.1 us
    unnamed x7, waiting for transfers between devices  73.8 us
    pmax x1, blocking collectives, body(): peaks = lax.pmax(jnp.max(jnp.abs(rotated), axis=1), 'seq')  33.4 us
    all_gather x1, waiting for transfers between devices, body(): lax.all_gather(grad_rot, 'tensor', axis=0, tiled=True)  30.4 us
    reduce_scatter x1, waiting for transfers between devices, body(): lax.psum_scatter(jnp.dot(block, rotation, preferred_element_type=jnp.floa...  29.1 us
  transfers between devices with their start and end apart: 7, of which 7 were waited for; matrix products, arithmetic and copies ran while one was open for 2% of the time, Pallas kernels for 0%

commit v1 on v0

v1 whole, which is shorter than its diff:
```python
import jax
import jax.numpy as jnp
from jax import lax
from jax.experimental import pallas as pl
from jax.experimental.pallas import tpu as pltpu
from jax.sharding import PartitionSpec as P

F32, BF16 = jnp.float32, jnp.bfloat16
ACT_CLIP = 0.5
NX, NY = 4, 4
TOK = 64
WIDE = 1024
SHARD = 128
PARTS = 2
PCOL = WIDE // PARTS
TILE = 256


def kernel(
    acts, incoming, rotation, weight, expos,
    total, grad_out,
    tok_a, tok_u, rot_v, w_v, quant, acts_t,
    prod_a, prod_u, core_a, core_u, send_a, send_u, recv_a, recv_u,
    own_a, own_u, peak_own, peak_recv, gate, grads,
    right_send, right_recv, left_send, left_recv,
    local_sem, gather_a_s, gather_a_r, gather_u_s, gather_u_r,
    core_s, core_r, ring_s, ring_r, peak_s, peak_r, grad_s, grad_r,
    right_s, right_r, left_s, left_r,
):
    n_sec = lax.axis_size("section")
    s = lax.axis_index("section")
    q = lax.axis_index("seq")
    t = lax.axis_index("tensor")
    zh, x = q // NX, q % NX
    y, c = t // 2, t % 2
    last = n_sec - 1

    def at_x(k):
        return (s, zh * NX + (x + k) % NX, t)

    def at_y(k):
        return (s, q, ((y + k) % NY) * 2 + c)

    far = (s, (1 - zh) * NX + x, t)
    mate = (s, q, y * 2 + 1 - c)
    up, down = (s + 1, q, t), (s - 1, q, t)

    def signal(device):
        pl.semaphore_signal(barrier, inc=1, device_id=device, device_id_type=pl.DeviceIdType.MESH)

    def send(src, dst, ssem, rsem, device):
        return pltpu.make_async_remote_copy(
            src_ref=src, dst_ref=dst, send_sem=ssem, recv_sem=rsem,
            device_id=device, device_id_type=pl.DeviceIdType.MESH,
        )

    def rows(block, size=TOK):
        return pl.ds(pl.multiple_of(block * size, size), size)

    load_rot = pltpu.make_async_copy(rotation, rot_v, local_sem.at[0])
    load_w = pltpu.make_async_copy(weight.at[0], w_v, local_sem.at[1])
    load_a = pltpu.make_async_copy(acts.at[0], tok_a.at[rows(q)], local_sem.at[2])
    load_u = pltpu.make_async_copy(incoming.at[0], tok_u.at[rows(q)], local_sem.at[3])
    load_a.start()
    load_w.start()
    load_rot.start()

    @pl.when(s == last)
    def _():
        load_u.start()

    barrier = pltpu.get_barrier_semaphore()
    for k in (1, 2, 3):
        signal(at_x(k))
        signal(at_y(k))
    signal(far)
    signal(mate)

    @pl.when(s < last)
    def _():
        signal(up)

    @pl.when(s > 0)
    def _():
        signal(down)

    pl.semaphore_wait(
        barrier, 8 + jnp.where(s < last, 1, 0) + jnp.where(s > 0, 1, 0)
    )

    mine, other = rows(q), rows((1 - zh) * NX + x)
    a_far = send(acts.at[0], tok_a.at[mine], gather_a_s.at[3], gather_a_r.at[3], far)
    a_near = [
        send(acts.at[0], tok_a.at[mine], gather_a_s.at[k - 1], gather_a_r.at[k - 1], at_x(k))
        for k in (1, 2, 3)
    ]
    a_pass = [
        send(tok_a.at[other], tok_a.at[other], gather_a_s.at[k + 3], gather_a_r.at[k + 3], at_x(k))
        for k in (1, 2, 3)
    ]
    u_shift = send(incoming.at[0], tok_u.at[mine], gather_u_s.at[7], gather_u_r.at[7], down)
    u_far = send(tok_u.at[mine], tok_u.at[mine], gather_u_s.at[3], gather_u_r.at[3], far)
    u_near = [
        send(tok_u.at[mine], tok_u.at[mine], gather_u_s.at[k - 1], gather_u_r.at[k - 1], at_x(k))
        for k in (1, 2, 3)
    ]
    u_pass = [
        send(tok_u.at[other], tok_u.at[other], gather_u_s.at[k + 3], gather_u_r.at[k + 3], at_x(k))
        for k in (1, 2, 3)
    ]

    @pl.when(s > 0)
    def _():
        u_shift.start()

    a_far.start()
    for copy in a_near:
        copy.start()

    @pl.when(s < last)
    def _():
        u_shift.wait_recv()

    @pl.when(s == last)
    def _():
        load_u.wait()

    u_far.start()
    for copy in u_near:
        copy.start()

    load_w.wait()
    scale = 127.0 * jnp.exp2(expos[...].astype(F32))
    inverse = 1.0 / scale

    def quantize(i, carry):
        r = rows(i, 64)
        quant[r] = (scale * jnp.tanh(w_v[r].astype(F32) * inverse)).astype(BF16)
        return carry

    lax.fori_loop(0, WIDE // 64, quantize, 0)
    load_rot.wait()
    load_a.wait()

    def project(half, tok, mat, flip, prod, core_in, base):
        r = pl.ds(pl.multiple_of(half * (NX * TOK), NX * TOK), NX * TOK)

        def tile(n, carry):
            cols = pl.ds(pl.multiple_of(n * TILE, TILE), TILE)
            if flip:
                part = lax.dot_general(
                    tok[r], mat[cols], (((1,), (1,)), ((), ())), preferred_element_type=F32
                )
            else:
                part = jnp.dot(tok[r], mat[:, cols], preferred_element_type=F32)
            prod[r, cols] = part.astype(BF16)
            return carry

        lax.fori_loop(0, WIDE // TILE, tile, 0)
        copies = []
        for j in (0, 1):
            chip = half * 2 + j
            copy = send(
                prod.at[rows(chip * 2 + 1 - c)], core_in.at[chip],
                core_s.at[base + j], core_r.at[base + j], mate,
            )
            copy.start()
            copies.append(copy)
        return copies

    def scatter(half, copies, prod, core_in, out, landing, own, base):
        for j in (0, 1):
            chip = half * 2 + j
            copies[j].wait_recv()
            both = prod[rows(chip * 2 + c)].astype(F32) + core_in[chip].astype(F32)

            @pl.when(chip == y)
            def _():
                own[...] = both

            @pl.when(chip != y)
            def _():
                k = (chip - y + NY) % NY - 1
                out[chip] = both.astype(BF16)
                send(
                    out.at[chip], landing.at[k], ring_s.at[base + k], ring_r.at[base + k],
                    (s, q, chip * 2 + c),
                ).start()

    def collect(out, landing, own, base):
        value = own[...]
        for k in range(3):
            send(out.at[0], landing.at[k], ring_s.at[base + k], ring_r.at[base + k], at_y(k + 1)).wait_recv()
            value = value + landing[k].astype(F32)
        return value

    near_half, far_half = zh, 1 - zh
    for copy in a_near:
        copy.wait_recv()
    ca_near = project(near_half, tok_a, rot_v, False, prod_a, core_a, 0)
    for copy in u_near:
        copy.wait_recv()
    cu_near = project(near_half, tok_u, quant, True, prod_u, core_u, 4)
    scatter(near_half, ca_near, prod_a, core_a, send_a, recv_a, own_a, 0)

    a_far.wait_recv()
    for copy in a_pass:
        copy.start()
    scatter(near_half, cu_near, prod_u, core_u, send_u, recv_u, own_u, 3)
    for copy in a_pass:
        copy.wait_recv()
    ca_far = project(far_half, tok_a, rot_v, False, prod_a, core_a, 2)
    scatter(far_half, ca_far, prod_a, core_a, send_a, recv_a, own_a, 0)

    u_far.wait_recv()
    for copy in u_pass:
        copy.start()

    rotated = collect(send_a, recv_a, own_a, 0)
    own_a[...] = rotated
    diagonal = lax.broadcasted_iota(jnp.int32, (TOK, 128), 0) == lax.broadcasted_iota(
        jnp.int32, (TOK, 128), 1
    )
    peak = jnp.max(jnp.abs(rotated), axis=1, keepdims=True)
    line = jnp.max(jnp.where(diagonal, peak, 0.0), axis=0, keepdims=True)
    peak_own[0] = jnp.broadcast_to(line, (8, 128))
    peak_x = [
        send(peak_own.at[0], peak_recv.at[k - 1], peak_s.at[k - 1], peak_r.at[k - 1], at_x(k))
        for k in (1, 2, 3)
    ]
    peak_z = send(peak_own.at[1], peak_recv.at[3], peak_s.at[3], peak_r.at[3], far)
    for copy in peak_x:
        copy.start()

    def turn(i, carry):
        r = pl.ds(pl.multiple_of(i * 128, 128), 128)
        acts_t[r] = tok_a[:, r].T
        return carry

    for copy in peak_x:
        copy.wait_recv()
    peak_own[1] = jnp.maximum(
        jnp.maximum(peak_own[0], peak_recv[0]), jnp.maximum(peak_recv[1], peak_recv[2])
    )
    peak_z.start()
    lax.fori_loop(0, WIDE // 128, turn, 0)
    for copy in u_pass:
        copy.wait_recv()
    cu_far = project(far_half, tok_u, quant, True, prod_u, core_u, 6)
    peak_z.wait_recv()
    line = jnp.maximum(peak_own[1], peak_recv[3])[0:1]
    peak = jnp.max(jnp.where(diagonal, line, 0.0), axis=1, keepdims=True)
    clip = ACT_CLIP * (peak + 1e-06)
    ratio = jnp.tanh(own_a[...] * (1.0 / clip))
    gate[...] = 1.0 - ratio * ratio
    scatter(far_half, cu_far, prod_u, core_u, send_u, recv_u, own_u, 3)
    back = collect(send_u, recv_u, own_u, 3)
    grad = (back * gate[...]).astype(BF16)
    grad_out[0] = grad
    grads[rows(t)] = grad

    g_y = [
        send(grads.at[rows(t)], grads.at[rows(t)], grad_s.at[k - 1], grad_r.at[k - 1], at_y(k))
        for k in (1, 2, 3)
    ]
    g_core = send(grads.at[rows(t)], grads.at[rows(t)], grad_s.at[3], grad_r.at[3], mate)
    g_pass = []
    for k in (1, 2, 3):
        block = rows(((y - k + NY) % NY) * 2 + c)
        g_pass.append(
            send(grads.at[block], grads.at[block], grad_s.at[3 + k], grad_r.at[3 + k], mate)
        )
    for copy in g_y:
        copy.start()
    g_core.start()
    for arrived, onward in zip(g_y, g_pass):
        arrived.wait_recv()
        onward.start()
    g_core.wait_recv()
    for copy in g_pass:
        copy.wait_recv()

    def partial(shard, p):
        return jnp.dot(
            acts_t[rows(shard, SHARD)], grads[:, p * PCOL : (p + 1) * PCOL],
            preferred_element_type=F32,
        )

    def hop(shard, p, out, landing, ssem, rsem, device):
        return send(
            out.at[shard, p], landing.at[shard, p], ssem.at[shard, p], rsem.at[shard, p], device
        )

    def step(tau, carry):
        for p in range(PARTS):

            @pl.when(tau >= s)
            def _():
                shard = last - (tau - s)
                value = partial(shard, p)
                copy = hop(shard, p, right_send, right_recv, right_s, right_r, up)

                @pl.when(s > 0)
                def _():
                    copy.wait_recv()
                    right_send[shard, p] = (value + right_recv[shard, p].astype(F32)).astype(BF16)

                @pl.when(s == 0)
                def _():
                    right_send[shard, p] = value.astype(BF16)

                copy.start()

            @pl.when(tau >= last - s)
            def _():
                shard = tau - (last - s)
                value = partial(shard, p)
                copy = hop(shard, p, left_send, left_recv, left_s, left_r, down)

                @pl.when(s < last)
                def _():
                    copy.wait_recv()
                    left_send[shard, p] = (value + left_recv[shard, p].astype(F32)).astype(BF16)

                @pl.when(s == last)
                def _():
                    left_send[shard, p] = value.astype(BF16)

                copy.start()

        return carry

    lax.fori_loop(0, last, step, 0)
    for p in range(PARTS):
        cols = slice(p * PCOL, (p + 1) * PCOL)
        total[:, cols] = partial(s, p)

        @pl.when(s > 0)
        def _():
            hop(s, p, right_send, right_recv, right_s, right_r, up).wait_recv()
            total[:, cols] = total[:, cols] + right_recv[s, p].astype(F32)

        @pl.when(s < last)
        def _():
            hop(s, p, left_send, left_recv, left_s, left_r, down).wait_recv()
            total[:, cols] = total[:, cols] + left_recv[s, p].astype(F32)

    for copy in a_near + [a_far] + a_pass + u_near + [u_far] + u_pass:
        copy.wait_send()

    @pl.when(s > 0)
    def _():
        u_shift.wait_send()

    for copy in ca_near + ca_far + cu_near + cu_far + peak_x + [peak_z] + g_y + [g_core] + g_pass:
        copy.wait_send()
    for k in range(3):
        send(send_a.at[0], recv_a.at[k], ring_s.at[k], ring_r.at[k], at_y(k + 1)).wait_send()
        send(send_u.at[0], recv_u.at[k], ring_s.at[3 + k], ring_r.at[3 + k], at_y(k + 1)).wait_send()

    def drain(shard, carry):
        for p in range(PARTS):

            @pl.when(shard > s)
            def _():
                hop(shard, p, right_send, right_recv, right_s, right_r, up).wait_send()

            @pl.when(shard < s)
            def _():
                hop(shard, p, left_send, left_recv, left_s, left_r, down).wait_send()

        return carry

    lax.fori_loop(0, n_sec, drain, 0)


def body(acts, incoming, rotation, q_weight, w_exponents):
    any_ref = pl.BlockSpec(memory_space=pl.ANY)
    vmem = pl.BlockSpec(memory_space=pltpu.VMEM)
    dma = pltpu.SemaphoreType.DMA
    n_sec = lax.axis_size("section")
    hops = (n_sec, PARTS, SHARD, PCOL)
    total, grad = pl.pallas_call(
        kernel,
        name="rotation_gradient",
        out_shape=(
            jax.ShapeDtypeStruct((SHARD, WIDE), F32),
            jax.ShapeDtypeStruct((1, TOK, WIDE), BF16),
        ),
        in_specs=[any_ref, any_ref, any_ref, any_ref, vmem],
        out_specs=(vmem, vmem),
        scratch_shapes=[
            pltpu.VMEM((8 * TOK, WIDE), BF16),
            pltpu.VMEM((8 * TOK, WIDE), BF16),
            pltpu.VMEM((WIDE, WIDE), BF16),
            pltpu.VMEM((WIDE, WIDE), BF16),
            pltpu.VMEM((WIDE, WIDE), BF16),
            pltpu.VMEM((WIDE, 8 * TOK), BF16),
            pltpu.VMEM((8 * TOK, WIDE), BF16),
            pltpu.VMEM((8 * TOK, WIDE), BF16),
            pltpu.VMEM((NY, TOK, WIDE), BF16),
            pltpu.VMEM((NY, TOK, WIDE), BF16),
            pltpu.VMEM((NY, TOK, WIDE), BF16),
            pltpu.VMEM((NY, TOK, WIDE), BF16),
            pltpu.VMEM((3, TOK, WIDE), BF16),
            pltpu.VMEM((3, TOK, WIDE), BF16),
            pltpu.VMEM((TOK, WIDE), F32),
            pltpu.VMEM((TOK, WIDE), F32),
            pltpu.VMEM((2, 8, 128), F32),
            pltpu.VMEM((4, 8, 128), F32),
            pltpu.VMEM((TOK, WIDE), F32),
            pltpu.VMEM((8 * TOK, WIDE), BF16),
            pltpu.VMEM(hops, BF16),
            pltpu.VMEM(hops, BF16),
            pltpu.VMEM(hops, BF16),
            pltpu.VMEM(hops, BF16),
            dma((4,)),
            dma((7,)), dma((7,)), dma((8,)), dma((8,)),
            dma((8,)), dma((8,)), dma((6,)), dma((6,)),
            dma((4,)), dma((4,)), dma((7,)), dma((7,)),
            dma((n_sec, PARTS)), dma((n_sec, PARTS)),
            dma((n_sec, PARTS)), dma((n_sec, PARTS)),
        ],
        compiler_params=pltpu.CompilerParams(
            collective_id=0, has_side_effects=True, vmem_limit_bytes=48 * 2**20
        ),
        cost_estimate=pl.CostEstimate(
            flops=3 * 2 * 512 * WIDE * WIDE, bytes_accessed=6 * 2**20, transcendentals=2**20
        ),
    )(acts, incoming, rotation, q_weight, w_exponents)
    return total, grad


def solution(mesh):
    placed = (
        P("section", "seq", "tensor"),
        P("section", "seq", "tensor"),
        P("tensor", "seq"),
        P("section", "seq", "tensor"),
        P("section", "tensor"),
    )
    return jax.shard_map(
        body,
        mesh=mesh,
        in_specs=placed,
        out_specs=(P(("tensor", "section"), "seq"), P("section", "tensor", "seq")),
        check_vma=False,
    )
```

time: 389 us -> 136 us (0.35)
  the two profiles are of different devices: /device:TPU:6 before, /device:TPU:96 now
where the time goes in v1:
time: 136 us
  Pallas kernels  128 us (94%)
  local copies, waits for them, and re-layouts  7.12 us (5%)
    pallas_call x1, Pallas kernels, body(): pl.pallas_call(kernel, name='rotation_gradient', out_shape=(jax.ShapeDtyp...  128 us
    unnamed x12, local copies, waits for them, and re-layouts  7.12 us

profile of v1, /device:TPU:96, one launch (start us, length us, event | category | flops | bytes accessed | tf_op | source)
XLA Modules:
  0.0 136.2 jit_solution(14346381371166492590)
XLA Ops:
  0.6 0.0 copy-start
  0.6 1.6 %copy-done = bf16[1024,1024]{1,0:T(8,128)(2,1)S(1)} copy-done((bf16[1024,1024]{1,0:T(8,128)(2,1)S(1)}, bf16[1024,1024]{1,0:T(8,128)(2,1)}, u32[]{:S(2)}) %copy-start) | copy-done | bytes 2097176
  2.2 0.0 copy-start.1
  2.2 1.6 %copy-done.1 = bf16[1,1024,1024]{2,1,0:T(8,128)(2,1)S(1)} copy-done((bf16[1,1024,1024]{2,1,0:T(8,128)(2,1)S(1)}, bf16[1,1024,1024]{2,1,0:T(8,128)(2,1)}, u32[]{:S(2)}) %copy-start.1) | copy-done | bytes 2097176
  3.8 0.0 copy-start.2
  3.8 0.9 copy-done.2
  4.7 0.0 copy-start.3
  4.7 0.9 copy-done.3
  5.6 0.0 copy-start.4
  5.6 0.7 copy-done.4
  6.3 128.4 %rotation_gradient.1 = (f32[128,1024]{1,0:T(8,128)S(1)}, bf16[1,64,1024]{2,1,0:T(8,128)(2,1)S(1)}) custom-call(bf16[1,64,1024]{2,1,0:T(8,128)(2,1)S(1)} %copy-done.2, bf16[1,64,1024]{2,1,0:T(8,128)(2,1)S(1)} %copy-done.3, bf16[1024,1024]{1,0:T(8,128)(2,1)S(1)} %copy-done, bf16[1,1024,1024]{2,1,0:T(8,128)(2,1)S(1)} %copy-done.1, s32[1,1024]{1,0:T(1,128)S(1)} %copy-done.4), custom_call_target="tpu_custom_call" | custom-call | flops 3221225472 | bytes 6291456 | tf_op jit(solution)/shard_map/rotation_gradient/pallas_call | solution.py:383
  134.7 0.8 copy.9
  135.5 0.7 copy.10
Async XLA Ops:
  0.6 1.6 %copy-start = (bf16[1024,1024]{1,0:T(8,128)(2,1)S(1)}, bf16[1024,1024]{1,0:T(8,128)(2,1)}, u32[]{:S(2)}) copy-start(bf16[1024,1024]{1,0:T(8,128)(2,1)} %rotation.1) | copy-start | bytes 6291460
  2.2 1.6 %copy-start.1 = (bf16[1,1024,1024]{2,1,0:T(8,128)(2,1)S(1)}, bf16[1,1024,1024]{2,1,0:T(8,128)(2,1)}, u32[]{:S(2)}) copy-start(bf16[1,1024,1024]{2,1,0:T(8,128)(2,1)} %weight.1) | copy-start | bytes 6291460
  3.8 0.9 copy-start.2
  4.7 0.9 copy-start.3
  5.6 0.7 copy-start.4

commit v2 on v1

v2 whole, which is shorter than its diff:
```python
import jax
import jax.numpy as jnp
from jax import lax
from jax.experimental import pallas as pl
from jax.experimental.pallas import tpu as pltpu
from jax.sharding import PartitionSpec as P

F32, BF16 = jnp.float32, jnp.bfloat16
ACT_CLIP = 0.5
NX, NY = 4, 4
TOK = 64
WIDE = 1024
SHARD = 128
PARTS = 2
PCOL = WIDE // PARTS
TILE = 256
HALF = TOK // 2


def kernel(
    acts, incoming, rotation, weight, expos,
    total, grad_out,
    tok_a, tok_u, rot_v, w_v, quant, acts_t,
    prod_a, prod_u, core_a, core_u, send_a, send_u, recv_a, recv_u,
    own_a, own_u, peak_own, peak_recv, gate, grads,
    right_send, right_recv, left_send, left_recv,
    local_sem, gather_a_s, gather_a_r, gather_u_s, gather_u_r,
    core_s, core_r, ring_s, ring_r, peak_s, peak_r, grad_s, grad_r,
    right_s, right_r, left_s, left_r,
):
    n_sec = lax.axis_size("section")
    s = lax.axis_index("section")
    q = lax.axis_index("seq")
    t = lax.axis_index("tensor")
    zh, x = q // NX, q % NX
    y, c = t // 2, t % 2
    last = n_sec - 1

    def at_x(k):
        return (s, zh * NX + (x + k) % NX, t)

    def at_y(k):
        return (s, q, ((y + k) % NY) * 2 + c)

    def at_far(k):
        return (s, (1 - zh) * NX + (x + k) % NX, t)

    far = at_far(0)
    mate = (s, q, y * 2 + 1 - c)
    up, down = (s + 1, q, t), (s - 1, q, t)

    def signal(device):
        pl.semaphore_signal(barrier, inc=1, device_id=device, device_id_type=pl.DeviceIdType.MESH)

    def send(src, dst, ssem, rsem, device):
        return pltpu.make_async_remote_copy(
            src_ref=src, dst_ref=dst, send_sem=ssem, recv_sem=rsem,
            device_id=device, device_id_type=pl.DeviceIdType.MESH,
        )

    def rows(block, size=TOK):
        return pl.ds(pl.multiple_of(block * size, size), size)

    load_rot = pltpu.make_async_copy(rotation, rot_v, local_sem.at[0])
    load_w = pltpu.make_async_copy(weight.at[0], w_v, local_sem.at[1])
    load_a = pltpu.make_async_copy(acts.at[0], tok_a.at[rows(q)], local_sem.at[2])
    load_u = pltpu.make_async_copy(incoming.at[0], tok_u.at[rows(q)], local_sem.at[3])
    load_a.start()
    load_w.start()
    load_rot.start()

    @pl.when(s == last)
    def _():
        load_u.start()

    barrier = pltpu.get_barrier_semaphore()
    for k in (1, 2, 3):
        signal(at_x(k))
        signal(at_y(k))
    for k in range(4):
        signal(at_far(k))
    signal(mate)

    @pl.when(s < last)
    def _():
        signal(up)

    @pl.when(s > 0)
    def _():
        signal(down)

    load_w.wait()
    scale = 127.0 * jnp.exp2(expos[...].astype(F32))
    inverse = 1.0 / scale

    def quantize(i, carry):
        r = rows(i, 64)
        quant[r] = (scale * jnp.tanh(w_v[r].astype(F32) * inverse)).astype(BF16)
        return carry

    lax.fori_loop(0, WIDE // 64, quantize, 0)
    pl.semaphore_wait(
        barrier, 11 + jnp.where(s < last, 1, 0) + jnp.where(s > 0, 1, 0)
    )

    mine = rows(q)

    def piece(block, h):
        return pl.ds(pl.multiple_of(block * TOK + h * HALF, HALF), HALF)

    def gather(first, tok, ssem, rsem):
        other = (1 - zh) * NX + x
        near = [
            send(first, tok.at[mine], ssem.at[k - 1], rsem.at[k - 1], at_x(k)) for k in (1, 2, 3)
        ]
        across = [
            send(
                first.at[pl.ds(h * HALF, HALF)], tok.at[piece(q, h)],
                ssem.at[3 + h], rsem.at[3 + h], far,
            )
            for h in (0, 1)
        ]
        onward = [
            [
                send(
                    tok.at[piece(other, h)], tok.at[piece(other, h)],
                    ssem.at[4 + 3 * h + k], rsem.at[4 + 3 * h + k], at_x(k),
                )
                for k in (1, 2, 3)
            ]
            for h in (0, 1)
        ]
        return near, across, onward

    a_near, a_far, a_pass = gather(acts.at[0], tok_a, gather_a_s, gather_a_r)
    u_near, u_far, u_pass = gather(tok_u.at[mine], tok_u, gather_u_s, gather_u_r)
    u_shift = send(incoming.at[0], tok_u.at[mine], gather_u_s.at[11], gather_u_r.at[11], down)

    def relay(arriving, onward):
        arriving.wait_recv()
        for copy in onward:
            copy.start()

    @pl.when(s > 0)
    def _():
        u_shift.start()

    a_far[0].start()
    for copy in a_near:
        copy.start()

    @pl.when(s < last)
    def _():
        u_shift.wait_recv()

    @pl.when(s == last)
    def _():
        load_u.wait()

    for copy in u_near:
        copy.start()

    load_rot.wait()
    load_a.wait()

    def follow(done, copy):
        done.wait_send()
        copy.start()

    every = (0, WIDE)
    parts = [(p * PCOL, PCOL) for p in range(PARTS)]

    def project(half, tok, mat, flip, prod, core_in, base, cols):
        r = pl.ds(pl.multiple_of(half * (NX * TOK), NX * TOK), NX * TOK)

        def tile(n, carry):
            at = pl.ds(pl.multiple_of(cols[0] + n * TILE, TILE), TILE)
            if flip:
                value = lax.dot_general(
                    tok[r], mat[at], (((1,), (1,)), ((), ())), preferred_element_type=F32
                )
            else:
                value = jnp.dot(tok[r], mat[:, at], preferred_element_type=F32)
            prod[r, at] = value.astype(BF16)
            return carry

        lax.fori_loop(0, cols[1] // TILE, tile, 0)
        copies = []
        for j in (0, 1):
            chip = half * 2 + j
            copy = send(
                prod.at[rows(chip * 2 + 1 - c), pl.ds(*cols)], core_in.at[chip, :, pl.ds(*cols)],
                core_s.at[base + j], core_r.at[base + j], mate,
            )
            copy.start()
            copies.append(copy)
        return copies

    def scatter(half, copies, prod, core_in, out, landing, own, base, cols):
        at = pl.ds(*cols)
        for j in (0, 1):
            chip = half * 2 + j
            copies[j].wait_recv()
            both = prod[rows(chip * 2 + c), at].astype(F32) + core_in[chip, :, at].astype(F32)

            @pl.when(chip == y)
            def _():
                own[:, at] = both

            @pl.when(chip != y)
            def _():
                k = (chip - y + NY) % NY - 1
                out[chip, :, at] = both.astype(BF16)
                send(
                    out.at[chip, :, at], landing.at[k, :, at],
                    ring_s.at[base + k], ring_r.at[base + k], (s, q, chip * 2 + c),
                ).start()

    def ring(k, out, landing, base, cols):
        at = pl.ds(*cols)
        return send(
            out.at[0, :, at], landing.at[k, :, at],
            ring_s.at[base + k], ring_r.at[base + k], at_y(k + 1),
        )

    def collect(out, landing, own, base, cols):
        at = pl.ds(*cols)
        value = own[:, at]
        for k in range(3):
            ring(k, out, landing, base, cols).wait_recv()
            value = value + landing[k, :, at].astype(F32)
        return value

    near_half, far_half = zh, 1 - zh
    def project_u(half, base):
        return [
            project(half, tok_u, quant, True, prod_u, core_u, base + 2 * p, parts[p])
            for p in range(PARTS)
        ]

    def scatter_u(half, copies):
        for p in range(PARTS):
            scatter(
                half, copies[p], prod_u, core_u, send_u, recv_u, own_u, 3 + 3 * p, parts[p]
            )

    follow(a_far[0], a_far[1])
    for copy in a_near:
        copy.wait_recv()
    ca_near = project(near_half, tok_a, rot_v, False, prod_a, core_a, 0, every)
    follow(a_far[1], u_far[0])
    relay(a_far[0], a_pass[0])
    for copy in u_near:
        copy.wait_recv()
    cu_near = project_u(near_half, 4)
    scatter(near_half, ca_near, prod_a, core_a, send_a, recv_a, own_a, 0, every)
    relay(a_far[1], a_pass[1])
    follow(u_far[0], u_far[1])
    scatter_u(near_half, cu_near)
    for copy in a_pass[0] + a_pass[1]:
        copy.wait_recv()
    ca_far = project(far_half, tok_a, rot_v, False, prod_a, core_a, 2, every)
    scatter(far_half, ca_far, prod_a, core_a, send_a, recv_a, own_a, 0, every)
    relay(u_far[0], u_pass[0])

    rotated = collect(send_a, recv_a, own_a, 0, every)
    own_a[...] = rotated
    diagonal = lax.broadcasted_iota(jnp.int32, (TOK, 128), 0) == lax.broadcasted_iota(
        jnp.int32, (TOK, 128), 1
    )
    peak = jnp.max(jnp.abs(rotated), axis=1, keepdims=True)
    line = jnp.max(jnp.where(diagonal, peak, 0.0), axis=0, keepdims=True)
    peak_own[...] = jnp.broadcast_to(line, (8, 128))
    peaks = [
        send(peak_own, peak_recv.at[i], peak_s.at[i], peak_r.at[i], device)
        for i, device in enumerate([at_x(k) for k in (1, 2, 3)] + [at_far(k) for k in range(4)])
    ]
    for copy in reversed(peaks):
        copy.start()
    relay(u_far[1], u_pass[1])

    def turn(i, carry):
        r = pl.ds(pl.multiple_of(i * 128, 128), 128)
        acts_t[r] = tok_a[:, r].T
        return carry

    lax.fori_loop(0, WIDE // 128, turn, 0)
    for copy in u_pass[0] + u_pass[1]:
        copy.wait_recv()
    cu_far = project_u(far_half, 8)
    scatter_u(far_half, cu_far)
    for copy in peaks:
        copy.wait_recv()
    line = jnp.maximum(peak_own[...], jnp.max(peak_recv[...], axis=0))[0:1]
    peak = jnp.max(jnp.where(diagonal, line, 0.0), axis=1, keepdims=True)
    clip = ACT_CLIP * (peak + 1e-06)
    ratio = jnp.tanh(own_a[...] * (1.0 / clip))
    gate[...] = 1.0 - ratio * ratio

    def part(block, p):
        return grads.at[rows(block), pl.ds(*parts[p])]

    g_y, g_core, g_pass = [], [], []
    for p in range(PARTS):
        at = pl.ds(*parts[p])
        back = collect(send_u, recv_u, own_u, 3 + 3 * p, parts[p])
        grad = (back * gate[:, at]).astype(BF16)
        grads[rows(t), at] = grad
        grad_out[0, :, at] = grad
        base = 7 * p
        g_y.append([
            send(part(t, p), part(t, p), grad_s.at[base + k], grad_r.at[base + k], at_y(k))
            for k in (1, 2, 3)
        ])
        g_core.append(send(part(t, p), part(t, p), grad_s.at[base], grad_r.at[base], mate))
        for copy in g_y[p] + [g_core[p]]:
            copy.start()
        passing = []
        for k in (1, 2, 3):
            block = ((y - k + NY) % NY) * 2 + c
            i = base + 3 + k
            passing.append(send(part(block, p), part(block, p), grad_s.at[i], grad_r.at[i], mate))
        g_pass.append(passing)

    def assemble(p):
        for arrived, onward in zip(g_y[p], g_pass[p]):
            arrived.wait_recv()
            onward.start()
        for copy in [g_core[p]] + g_pass[p]:
            copy.wait_recv()

    def partial(shard, p):
        return jnp.dot(
            acts_t[rows(shard, SHARD)], grads[:, p * PCOL : (p + 1) * PCOL],
            preferred_element_type=F32,
        )

    def hop(shard, p, out, landing, ssem, rsem, device):
        return send(
            out.at[shard, p], landing.at[shard, p], ssem.at[shard, p], rsem.at[shard, p], device
        )

    def step(tau, p):
        @pl.when(tau >= s)
        def _():
            shard = last - (tau - s)
            value = partial(shard, p)
            copy = hop(shard, p, right_send, right_recv, right_s, right_r, up)

            @pl.when(s > 0)
            def _():
                copy.wait_recv()
                right_send[shard, p] = (value + right_recv[shard, p].astype(F32)).astype(BF16)

            @pl.when(s == 0)
            def _():
                right_send[shard, p] = value.astype(BF16)

            copy.start()

        @pl.when(tau >= last - s)
        def _():
            shard = tau - (last - s)
            value = partial(shard, p)
            copy = hop(shard, p, left_send, left_recv, left_s, left_r, down)

            @pl.when(s < last)
            def _():
                copy.wait_recv()
                left_send[shard, p] = (value + left_recv[shard, p].astype(F32)).astype(BF16)

            @pl.when(s == last)
            def _():
                left_send[shard, p] = value.astype(BF16)

            copy.start()

    assemble(0)
    step(0, 0)
    assemble(1)
    step(0, 1)

    def steps(tau, carry):
        for p in range(PARTS):
            step(tau, p)
        return carry

    lax.fori_loop(1, last, steps, 0)
    for p in range(PARTS):
        cols = slice(p * PCOL, (p + 1) * PCOL)
        total[:, cols] = partial(s, p)

        @pl.when(s > 0)
        def _():
            hop(s, p, right_send, right_recv, right_s, right_r, up).wait_recv()
            total[:, cols] = total[:, cols] + right_recv[s, p].astype(F32)

        @pl.when(s < last)
        def _():
            hop(s, p, left_send, left_recv, left_s, left_r, down).wait_recv()
            total[:, cols] = total[:, cols] + left_recv[s, p].astype(F32)

    for copy in a_pass[0] + a_pass[1] + u_near + u_far[1:] + u_pass[0] + u_pass[1]:
        copy.wait_send()

    @pl.when(s > 0)
    def _():
        u_shift.wait_send()

    for copy in a_near + ca_far + sum(cu_near + cu_far, ca_near) + peaks:
        copy.wait_send()
    for p in range(PARTS):
        for copy in g_y[p] + [g_core[p]] + g_pass[p]:
            copy.wait_send()
    for k in range(3):
        ring(k, send_a, recv_a, 0, every).wait_send()
        for p in range(PARTS):
            ring(k, send_u, recv_u, 3 + 3 * p, parts[p]).wait_send()

    def drain(shard, carry):
        for p in range(PARTS):

            @pl.when(shard > s)
            def _():
                hop(shard, p, right_send, right_recv, right_s, right_r, up).wait_send()

            @pl.when(shard < s)
            def _():
                hop(shard, p, left_send, left_recv, left_s, left_r, down).wait_send()

        return carry

    lax.fori_loop(0, n_sec, drain, 0)


def body(acts, incoming, rotation, q_weight, w_exponents):
    hbm = pl.BlockSpec(memory_space=pltpu.HBM)
    vmem = pl.BlockSpec(memory_space=pltpu.VMEM)
    dma = pltpu.SemaphoreType.DMA
    n_sec = lax.axis_size("section")
    hops = (n_sec, PARTS, SHARD, PCOL)
    total, grad = pl.pallas_call(
        kernel,
        name="rotation_gradient",
        out_shape=(
            jax.ShapeDtypeStruct((SHARD, WIDE), F32),
            jax.ShapeDtypeStruct((1, TOK, WIDE), BF16),
        ),
        in_specs=[hbm, hbm, hbm, hbm, vmem],
        out_specs=(vmem, vmem),
        scratch_shapes=[
            pltpu.VMEM((8 * TOK, WIDE), BF16),
            pltpu.VMEM((8 * TOK, WIDE), BF16),
            pltpu.VMEM((WIDE, WIDE), BF16),
            pltpu.VMEM((WIDE, WIDE), BF16),
            pltpu.VMEM((WIDE, WIDE), BF16),
            pltpu.VMEM((WIDE, 8 * TOK), BF16),
            pltpu.VMEM((8 * TOK, WIDE), BF16),
            pltpu.VMEM((8 * TOK, WIDE), BF16),
            pltpu.VMEM((NY, TOK, WIDE), BF16),
            pltpu.VMEM((NY, TOK, WIDE), BF16),
            pltpu.VMEM((NY, TOK, WIDE), BF16),
            pltpu.VMEM((NY, TOK, WIDE), BF16),
            pltpu.VMEM((3, TOK, WIDE), BF16),
            pltpu.VMEM((3, TOK, WIDE), BF16),
            pltpu.VMEM((TOK, WIDE), F32),
            pltpu.VMEM((TOK, WIDE), F32),
            pltpu.VMEM((8, 128), F32),
            pltpu.VMEM((7, 8, 128), F32),
            pltpu.VMEM((TOK, WIDE), F32),
            pltpu.VMEM((8 * TOK, WIDE), BF16),
            pltpu.VMEM(hops, BF16),
            pltpu.VMEM(hops, BF16),
            pltpu.VMEM(hops, BF16),
            pltpu.VMEM(hops, BF16),
            dma((4,)),
            dma((11,)), dma((11,)), dma((12,)), dma((12,)),
            dma((12,)), dma((12,)), dma((3 + 3 * PARTS,)), dma((3 + 3 * PARTS,)),
            dma((7,)), dma((7,)), dma((7 * PARTS,)), dma((7 * PARTS,)),
            dma((n_sec, PARTS)), dma((n_sec, PARTS)),
            dma((n_sec, PARTS)), dma((n_sec, PARTS)),
        ],
        compiler_params=pltpu.CompilerParams(
            collective_id=0, has_side_effects=True, vmem_limit_bytes=63 * 2**20
        ),
        cost_estimate=pl.CostEstimate(
            flops=3 * 2 * 512 * WIDE * WIDE, bytes_accessed=6 * 2**20, transcendentals=2**20
        ),
    )(acts, incoming, rotation, q_weight, w_exponents)
    return total, grad


def solution(mesh):
    placed = (
        P("section", "seq", "tensor"),
        P("section", "seq", "tensor"),
        P("tensor", "seq"),
        P("section", "seq", "tensor"),
        P("section", "tensor"),
    )
    return jax.shard_map(
        body,
        mesh=mesh,
        in_specs=placed,
        out_specs=(P(("tensor", "section"), "seq"), P("section", "tensor", "seq")),
        check_vma=False,
    )
```

time: 136 us -> 118 us (0.87)
  the two profiles are of different devices: /device:TPU:96 before, /device:TPU:449 now
where the time goes in v2:
time: 118 us
  Pallas kernels  113 us (96%)
  local copies, waits for them, and re-layouts  3.45 us (3%)
    pallas_call x1, Pallas kernels, body(): pl.pallas_call(kernel, name='rotation_gradient', out_shape=(jax.ShapeDtyp...  113 us
    unnamed x2, local copies, waits for them, and re-layouts  3.45 us

profile of v2, /device:TPU:449, one launch (start us, length us, event | category | flops | bytes accessed | tf_op | source)
XLA Modules:
  0.0 117.5 jit_solution(4720543260786674035)
XLA Ops:
  0.6 113.4 %rotation_gradient.1 = (f32[128,1024]{1,0:T(8,128)}, bf16[1,64,1024]{2,1,0:T(8,128)(2,1)}) custom-call(bf16[1,64,1024]{2,1,0:T(8,128)(2,1)} %acts.1, bf16[1,64,1024]{2,1,0:T(8,128)(2,1)} %incoming.1, bf16[1024,1024]{1,0:T(8,128)(2,1)} %rotation.1, bf16[1,1024,1024]{2,1,0:T(8,128)(2,1)} %weight.1, s32[1,1024]{1,0:T(1,128)} %expos.1), custom_call_target="tpu_custom_call" | custom-call | flops 3221225472 | bytes 6291456 | tf_op jit(solution)/shard_map/rotation_gradient/pallas_call | solution.py:442
  114.1 1.9 %copy.9 = f32[128,1024]{1,0:T(8,128)} copy(f32[128,1024]{1,0:T(8,128)} %get-tuple-element.4) | data formatting | bytes 1048576
  116.0 1.6 %copy.10 = bf16[1,64,1024]{2,1,0:T(8,128)(2,1)} copy(bf16[1,64,1024]{2,1,0:T(8,128)(2,1)} %get-tuple-element.5) | data formatting | bytes 262144

commit v3 on v2

--- a/solution.py
+++ b/solution.py
@@ -7,11 +7,12 @@
 
 F32, BF16 = jnp.float32, jnp.bfloat16
 ACT_CLIP = 0.5
+VMEM_LIMIT = 63 * 2**20
 NX, NY = 4, 4
 TOK = 64
 WIDE = 1024
 SHARD = 128
-PARTS = 2
+PARTS = 4
 PCOL = WIDE // PARTS
 TILE = 256
 HALF = TOK // 2
@@ -167,108 +168,116 @@
         done.wait_send()
         copy.start()
 
-    every = (0, WIDE)
     parts = [(p * PCOL, PCOL) for p in range(PARTS)]
 
-    def project(half, tok, mat, flip, prod, core_in, base, cols):
-        r = pl.ds(pl.multiple_of(half * (NX * TOK), NX * TOK), NX * TOK)
+    def project(half, h, tok, mat, flip, prod, core_in, base):
+        value = jnp.concatenate([tok[piece(half * NX + i, h)] for i in range(NX)], axis=0)
 
         def tile(n, carry):
-            at = pl.ds(pl.multiple_of(cols[0] + n * TILE, TILE), TILE)
+            at = pl.ds(pl.multiple_of(n * TILE, TILE), TILE)
             if flip:
-                value = lax.dot_general(
-                    tok[r], mat[at], (((1,), (1,)), ((), ())), preferred_element_type=F32
+                result = lax.dot_general(
+                    value, mat[at], (((1,), (1,)), ((), ())), preferred_element_type=F32
                 )
             else:
-                value = jnp.dot(tok[r], mat[:, at], preferred_element_type=F32)
-            prod[r, at] = value.astype(BF16)
+                result = jnp.dot(value, mat[:, at], preferred_element_type=F32)
+            for i in range(NX):
+                prod[piece(half * NX + i, h), at] = result[i * HALF : (i + 1) * HALF].astype(BF16)
             return carry
 
-        lax.fori_loop(0, cols[1] // TILE, tile, 0)
+        lax.fori_loop(0, WIDE // TILE, tile, 0)
         copies = []
         for j in (0, 1):
             chip = half * 2 + j
             copy = send(
-                prod.at[rows(chip * 2 + 1 - c), pl.ds(*cols)], core_in.at[chip, :, pl.ds(*cols)],
+                prod.at[piece(chip * 2 + 1 - c, h)], core_in.at[chip, pl.ds(h * HALF, HALF)],
                 core_s.at[base + j], core_r.at[base + j], mate,
             )
             copy.start()
             copies.append(copy)
         return copies
 
-    def scatter(half, copies, prod, core_in, out, landing, own, base, cols):
-        at = pl.ds(*cols)
+    def scatter(half, h, copies, prod, core_in, out, landing, own, base):
+        at = pl.ds(h * HALF, HALF)
         for j in (0, 1):
             chip = half * 2 + j
             copies[j].wait_recv()
-            both = prod[rows(chip * 2 + c), at].astype(F32) + core_in[chip, :, at].astype(F32)
+            both = prod[piece(chip * 2 + c, h)].astype(F32) + core_in[chip, at].astype(F32)
 
             @pl.when(chip == y)
             def _():
-                own[:, at] = both
+                own[at] = both
 
             @pl.when(chip != y)
             def _():
                 k = (chip - y + NY) % NY - 1
-                out[chip, :, at] = both.astype(BF16)
+                out[chip, at] = both.astype(BF16)
                 send(
-                    out.at[chip, :, at], landing.at[k, :, at],
+                    out.at[chip, at], landing.at[k, at],
                     ring_s.at[base + k], ring_r.at[base + k], (s, q, chip * 2 + c),
                 ).start()
 
-    def ring(k, out, landing, base, cols):
-        at = pl.ds(*cols)
+    def ring(k, h, out, landing, base):
+        at = pl.ds(h * HALF, HALF)
         return send(
-            out.at[0, :, at], landing.at[k, :, at],
+            out.at[0, at], landing.at[k, at],
             ring_s.at[base + k], ring_r.at[base + k], at_y(k + 1),
         )
 
-    def collect(out, landing, own, base, cols):
-        at = pl.ds(*cols)
-        value = own[:, at]
+    def collect(out, landing, own, base):
+        value = own[...]
         for k in range(3):
-            ring(k, out, landing, base, cols).wait_recv()
-            value = value + landing[k, :, at].astype(F32)
+            for h in (0, 1):
+                ring(k, h, out, landing, base + 3 * h).wait_recv()
+            value = value + landing[k].astype(F32)
         return value
 
     near_half, far_half = zh, 1 - zh
-    def project_u(half, base):
-        return [
-            project(half, tok_u, quant, True, prod_u, core_u, base + 2 * p, parts[p])
-            for p in range(PARTS)
-        ]
-
-    def scatter_u(half, copies):
-        for p in range(PARTS):
-            scatter(
-                half, copies[p], prod_u, core_u, send_u, recv_u, own_u, 3 + 3 * p, parts[p]
-            )
+
+    def project_a(half, h, base):
+        return project(half, h, tok_a, rot_v, False, prod_a, core_a, base)
+
+    def project_u(half, h, base):
+        return project(half, h, tok_u, quant, True, prod_u, core_u, base)
+
+    def scatter_a(half, h, copies):
+        scatter(half, h, copies, prod_a, core_a, send_a, recv_a, own_a, 3 * h)
+
+    def scatter_u(half, h, copies):
+        scatter(half, h, copies, prod_u, core_u, send_u, recv_u, own_u, 6 + 3 * h)
+
+    def arrive(copies):
+        for copy in copies:
+            copy.wait_recv()
 
     follow(a_far[0], a_far[1])
-    for copy in a_near:
-        copy.wait_recv()
-    ca_near = project(near_half, tok_a, rot_v, False, prod_a, core_a, 0, every)
+    arrive(a_near)
+    mates = [project_a(near_half, 0, 0), project_a(near_half, 1, 2)]
     follow(a_far[1], u_far[0])
     relay(a_far[0], a_pass[0])
-    for copy in u_near:
-        copy.wait_recv()
-    cu_near = project_u(near_half, 4)
-    scatter(near_half, ca_near, prod_a, core_a, send_a, recv_a, own_a, 0, every)
+    scatter_a(near_half, 0, mates[0])
+    scatter_a(near_half, 1, mates[1])
+    arrive(u_near)
+    mates += [project_u(near_half, 0, 8), project_u(near_half, 1, 10)]
+    arrive(a_pass[0])
+    mates.append(project_a(far_half, 0, 4))
     relay(a_far[1], a_pass[1])
     follow(u_far[0], u_far[1])
-    scatter_u(near_half, cu_near)
-    for copy in a_pass[0] + a_pass[1]:
-        copy.wait_recv()
-    ca_far = project(far_half, tok_a, rot_v, False, prod_a, core_a, 2, every)
-    scatter(far_half, ca_far, prod_a, core_a, send_a, recv_a, own_a, 0, every)
+    scatter_a(far_half, 0, mates[4])
+    scatter_u(near_half, 0, mates[2])
+    scatter_u(near_half, 1, mates[3])
+    arrive(a_pass[1])
+    mates.append(project_a(far_half, 1, 6))
     relay(u_far[0], u_pass[0])
-
-    rotated = collect(send_a, recv_a, own_a, 0, every)
+    scatter_a(far_half, 1, mates[5])
+    relay(u_far[1], u_pass[1])
+
+    rotated = collect(send_a, recv_a, own_a, 0)
     own_a[...] = rotated
+    peak = jnp.max(jnp.abs(rotated), axis=1, keepdims=True)
     diagonal = lax.broadcasted_iota(jnp.int32, (TOK, 128), 0) == lax.broadcasted_iota(
         jnp.int32, (TOK, 128), 1
     )
-    peak = jnp.max(jnp.abs(rotated), axis=1, keepdims=True)
     line = jnp.max(jnp.where(diagonal, peak, 0.0), axis=0, keepdims=True)
     peak_own[...] = jnp.broadcast_to(line, (8, 128))
     peaks = [
@@ -277,7 +286,10 @@
     ]
     for copy in reversed(peaks):
         copy.start()
-    relay(u_far[1], u_pass[1])
+    for h in (0, 1):
+        arrive(u_pass[h])
+        mates.append(project_u(far_half, h, 12 + 2 * h))
+        scatter_u(far_half, h, mates[-1])
 
     def turn(i, carry):
         r = pl.ds(pl.multiple_of(i * 128, 128), 128)
@@ -285,10 +297,6 @@
         return carry
 
     lax.fori_loop(0, WIDE // 128, turn, 0)
-    for copy in u_pass[0] + u_pass[1]:
-        copy.wait_recv()
-    cu_far = project_u(far_half, 8)
-    scatter_u(far_half, cu_far)
     for copy in peaks:
         copy.wait_recv()
     line = jnp.maximum(peak_own[...], jnp.max(peak_recv[...], axis=0))[0:1]
@@ -300,11 +308,11 @@
     def part(block, p):
         return grads.at[rows(block), pl.ds(*parts[p])]
 
+    back = collect(send_u, recv_u, own_u, 6)
     g_y, g_core, g_pass = [], [], []
     for p in range(PARTS):
         at = pl.ds(*parts[p])
-        back = collect(send_u, recv_u, own_u, 3 + 3 * p, parts[p])
-        grad = (back * gate[:, at]).astype(BF16)
+        grad = (back[:, p * PCOL : (p + 1) * PCOL] * gate[:, at]).astype(BF16)
         grads[rows(t), at] = grad
         grad_out[0, :, at] = grad
         base = 7 * p
@@ -375,10 +383,9 @@
 
             copy.start()
 
-    assemble(0)
-    step(0, 0)
-    assemble(1)
-    step(0, 1)
+    for p in range(PARTS):
+        assemble(p)
+        step(0, p)
 
     def steps(tau, carry):
         for p in range(PARTS):
@@ -407,15 +414,15 @@
     def _():
         u_shift.wait_send()
 
-    for copy in a_near + ca_far + sum(cu_near + cu_far, ca_near) + peaks:
+    for copy in a_near + sum(mates, peaks):
         copy.wait_send()
     for p in range(PARTS):
         for copy in g_y[p] + [g_core[p]] + g_pass[p]:
             copy.wait_send()
     for k in range(3):
-        ring(k, send_a, recv_a, 0, every).wait_send()
-        for p in range(PARTS):
-            ring(k, send_u, recv_u, 3 + 3 * p, parts[p]).wait_send()
+        for h in (0, 1):
+            ring(k, h, send_a, recv_a, 3 * h).wait_send()
+            ring(k, h, send_u, recv_u, 6 + 3 * h).wait_send()
 
     def drain(shard, carry):
         for p in range(PARTS):
@@ -475,13 +482,13 @@
             pltpu.VMEM(hops, BF16),
             dma((4,)),
             dma((11,)), dma((11,)), dma((12,)), dma((12,)),
-            dma((12,)), dma((12,)), dma((3 + 3 * PARTS,)), dma((3 + 3 * PARTS,)),
+            dma((16,)), dma((16,)), dma((12,)), dma((12,)),
             dma((7,)), dma((7,)), dma((7 * PARTS,)), dma((7 * PARTS,)),
             dma((n_sec, PARTS)), dma((n_sec, PARTS)),
             dma((n_sec, PARTS)), dma((n_sec, PARTS)),
         ],
         compiler_params=pltpu.CompilerParams(
-            collective_id=0, has_side_effects=True, vmem_limit_bytes=63 * 2**20
+            collective_id=0, has_side_effects=True, vmem_limit_bytes=VMEM_LIMIT
         ),
         cost_estimate=pl.CostEstimate(
             flops=3 * 2 * 512 * WIDE * WIDE, bytes_accessed=6 * 2**20, transcendentals=2**20

time: 118 us -> 115 us (0.975)
  the two profiles are of different devices: /device:TPU:449 before, /device:TPU:464 now
where the time goes in v3:
time: 115 us
  Pallas kernels  111 us (97%)
  local copies, waits for them, and re-layouts  3.45 us (3%)
    pallas_call x1, Pallas kernels, body(): pl.pallas_call(kernel, name='rotation_gradient', out_shape=(jax.ShapeDtyp...  111 us
    unnamed x2, local copies, waits for them, and re-layouts  3.45 us

profile of v3, /device:TPU:464, one launch (start us, length us, event | category | flops | bytes accessed | tf_op | source)
XLA Modules:
  0.0 114.8 jit_solution(4268303576752788902)
XLA Ops:
  0.6 110.7 %rotation_gradient.1 = (f32[128,1024]{1,0:T(8,128)}, bf16[1,64,1024]{2,1,0:T(8,128)(2,1)}) custom-call(bf16[1,64,1024]{2,1,0:T(8,128)(2,1)} %acts.1, bf16[1,64,1024]{2,1,0:T(8,128)(2,1)} %incoming.1, bf16[1024,1024]{1,0:T(8,128)(2,1)} %rotation.1, bf16[1,1024,1024]{2,1,0:T(8,128)(2,1)} %weight.1, s32[1,1024]{1,0:T(1,128)} %expos.1), custom_call_target="tpu_custom_call" | custom-call | flops 3221225472 | bytes 6291456 | tf_op jit(solution)/shard_map/rotation_gradient/pallas_call | solution.py:449
  111.4 1.9 %copy.9 = f32[128,1024]{1,0:T(8,128)} copy(f32[128,1024]{1,0:T(8,128)} %get-tuple-element.4) | data formatting | bytes 1048576
  113.3 1.6 %copy.10 = bf16[1,64,1024]{2,1,0:T(8,128)(2,1)} copy(bf16[1,64,1024]{2,1,0:T(8,128)(2,1)} %get-tuple-element.5) | data formatting | bytes 262144

commit v4 on v3

--- a/solution.py
+++ b/solution.py
@@ -20,8 +20,8 @@
 
 def kernel(
     acts, incoming, rotation, weight, expos,
-    total, grad_out,
-    tok_a, tok_u, rot_v, w_v, quant, acts_t,
+    total_out, grad_out,
+    total, tok_a, tok_u, rot_v, w_v, quant, acts_t,
     prod_a, prod_u, core_a, core_u, send_a, send_u, recv_a, recv_u,
     own_a, own_u, peak_own, peak_recv, gate, grads,
     right_send, right_recv, left_send, left_recv,
@@ -314,7 +314,6 @@
         at = pl.ds(*parts[p])
         grad = (back[:, p * PCOL : (p + 1) * PCOL] * gate[:, at]).astype(BF16)
         grads[rows(t), at] = grad
-        grad_out[0, :, at] = grad
         base = 7 * p
         g_y.append([
             send(part(t, p), part(t, p), grad_s.at[base + k], grad_r.at[base + k], at_y(k))
@@ -330,6 +329,9 @@
             passing.append(send(part(block, p), part(block, p), grad_s.at[i], grad_r.at[i], mate))
         g_pass.append(passing)
 
+    store_grad = pltpu.make_async_copy(grads.at[rows(t)], grad_out.at[0], local_sem.at[4])
+    store_grad.start()
+
     def assemble(p):
         for arrived, onward in zip(g_y[p], g_pass[p]):
             arrived.wait_recv()
@@ -393,8 +395,9 @@
         return carry
 
     lax.fori_loop(1, last, steps, 0)
+    stores = []
     for p in range(PARTS):
-        cols = slice(p * PCOL, (p + 1) * PCOL)
+        cols = pl.ds(*parts[p])
         total[:, cols] = partial(s, p)
 
         @pl.when(s > 0)
@@ -406,6 +409,9 @@
         def _():
             hop(s, p, left_send, left_recv, left_s, left_r, down).wait_recv()
             total[:, cols] = total[:, cols] + left_recv[s, p].astype(F32)
+
+        stores.append(pltpu.make_async_copy(total.at[:, cols], total_out.at[:, cols], local_sem.at[5 + p]))
+        stores[p].start()
 
     for copy in a_pass[0] + a_pass[1] + u_near + u_far[1:] + u_pass[0] + u_pass[1]:
         copy.wait_send()
@@ -438,6 +444,27 @@
         return carry
 
     lax.fori_loop(0, n_sec, drain, 0)
+    for store in [store_grad] + stores:
+        store.wait()
+
+
+def hand_on(total, grad, total_out, grad_out, total_v, grad_v, in_sem, out_sem):
+    quarters = [pl.ds(i * (SHARD // 4), SHARD // 4) for i in range(4)]
+    loads = [
+        pltpu.make_async_copy(total.at[r], total_v.at[r], in_sem.at[i])
+        for i, r in enumerate(quarters)
+    ] + [pltpu.make_async_copy(grad, grad_v, in_sem.at[4])]
+    stores = [
+        pltpu.make_async_copy(total_v.at[r], total_out.at[r], out_sem.at[i])
+        for i, r in enumerate(quarters)
+    ] + [pltpu.make_async_copy(grad_v, grad_out, out_sem.at[4])]
+    for load in loads:
+        load.start()
+    for load, store in zip(loads, stores):
+        load.wait()
+        store.start()
+    for store in stores:
+        store.wait()
 
 
 def body(acts, incoming, rotation, q_weight, w_exponents):
@@ -454,8 +481,9 @@
             jax.ShapeDtypeStruct((1, TOK, WIDE), BF16),
         ),
         in_specs=[hbm, hbm, hbm, hbm, vmem],
-        out_specs=(vmem, vmem),
+        out_specs=(hbm, hbm),
         scratch_shapes=[
+            pltpu.VMEM((SHARD, WIDE), F32),
             pltpu.VMEM((8 * TOK, WIDE), BF16),
             pltpu.VMEM((8 * TOK, WIDE), BF16),
             pltpu.VMEM((WIDE, WIDE), BF16),
@@ -480,7 +508,7 @@
             pltpu.VMEM(hops, BF16),
             pltpu.VMEM(hops, BF16),
             pltpu.VMEM(hops, BF16),
-            dma((4,)),
+            dma((5 + PARTS,)),
             dma((11,)), dma((11,)), dma((12,)), dma((12,)),
             dma((16,)), dma((16,)), dma((12,)), dma((12,)),
             dma((7,)), dma((7,)), dma((7 * PARTS,)), dma((7 * PARTS,)),
@@ -494,7 +522,22 @@
             flops=3 * 2 * 512 * WIDE * WIDE, bytes_accessed=6 * 2**20, transcendentals=2**20
         ),
     )(acts, incoming, rotation, q_weight, w_exponents)
-    return total, grad
+    return pl.pallas_call(
+        hand_on,
+        name="results",
+        out_shape=(
+            jax.ShapeDtypeStruct((SHARD, WIDE), F32),
+            jax.ShapeDtypeStruct((1, TOK, WIDE), BF16),
+        ),
+        in_specs=[hbm, hbm],
+        out_specs=(hbm, hbm),
+        scratch_shapes=[
+            pltpu.VMEM((SHARD, WIDE), F32),
+            pltpu.VMEM((1, TOK, WIDE), BF16),
+            dma((5,)), dma((5,)),
+        ],
+        compiler_params=pltpu.CompilerParams(vmem_limit_bytes=VMEM_LIMIT),
+    )(total, grad)
 
 
 def solution(mesh):

time: 115 us -> 113 us (0.983)
  local copies, waits for them, and re-layouts: 3.45 us -> 0 us
    unnamed x2 -> x0, local copies, waits for them, and re-layouts: 3.45 us -> none
    pallas_call x0 -> x1, Pallas kernels: none -> 1.91 us  [body(): pl.pallas_call(hand_on, name='results', out_shape=(jax.ShapeDtypeStruct((...]
where the time goes in v4:
time: 113 us
  Pallas kernels  112 us (99%)
    pallas_call x1, Pallas kernels, body(): pl.pallas_call(kernel, name='rotation_gradient', out_shape=(jax.ShapeDtyp...  110 us

profile of v4, /device:TPU:464, one launch (start us, length us, event | category | flops | bytes accessed | tf_op | source)
XLA Modules:
  0.0 112.9 jit_solution(18004683488575539729)
XLA Ops:
  0.6 110.4 %rotation_gradient.1 = (f32[128,1024]{1,0:T(8,128)}, bf16[1,64,1024]{2,1,0:T(8,128)(2,1)}) custom-call(bf16[1,64,1024]{2,1,0:T(8,128)(2,1)} %acts.1, bf16[1,64,1024]{2,1,0:T(8,128)(2,1)} %incoming.1, bf16[1024,1024]{1,0:T(8,128)(2,1)} %rotation.1, bf16[1,1024,1024]{2,1,0:T(8,128)(2,1)} %weight.1, s32[1,1024]{1,0:T(1,128)} %expos.1), custom_call_target="tpu_custom_call" | custom-call | flops 3221225472 | bytes 6291456 | tf_op jit(solution)/shard_map/rotation_gradient/pallas_call | solution.py:476
  111.0 1.9 %results.1 = (f32[128,1024]{1,0:T(8,128)}, bf16[1,64,1024]{2,1,0:T(8,128)(2,1)}) custom-call(f32[128,1024]{1,0:T(8,128)} %get-tuple-element.4.total, bf16[1,64,1024]{2,1,0:T(8,128)(2,1)} %get-tuple-element.5.grad), custom_call_target="tpu_custom_call" | custom-call | tf_op jit(solution)/shard_map/results/pallas_call | solution.py:525

commit v5 on v4

--- a/solution.py
+++ b/solution.py
@@ -12,7 +12,7 @@
 TOK = 64
 WIDE = 1024
 SHARD = 128
-PARTS = 4
+PARTS = 8
 PCOL = WIDE // PARTS
 TILE = 256
 HALF = TOK // 2

time: 113 us -> 117 us (1.035)
  the two profiles are of different devices: /device:TPU:464 before, /device:TPU:448 now
where the time goes in v5:
time: 117 us
  Pallas kernels  116 us (99%)
    pallas_call x1, Pallas kernels, body(): pl.pallas_call(kernel, name='rotation_gradient', out_shape=(jax.ShapeDtyp...  114 us

profile of v5, /device:TPU:448, one launch (start us, length us, event | category | flops | bytes accessed | tf_op | source)
XLA Modules:
  0.0 116.9 jit_solution(5964127056990763707)
XLA Ops:
  0.6 114.4 %rotation_gradient.1 = (f32[128,1024]{1,0:T(8,128)}, bf16[1,64,1024]{2,1,0:T(8,128)(2,1)}) custom-call(bf16[1,64,1024]{2,1,0:T(8,128)(2,1)} %acts.1, bf16[1,64,1024]{2,1,0:T(8,128)(2,1)} %incoming.1, bf16[1024,1024]{1,0:T(8,128)(2,1)} %rotation.1, bf16[1,1024,1024]{2,1,0:T(8,128)(2,1)} %weight.1, s32[1,1024]{1,0:T(1,128)} %expos.1), custom_call_target="tpu_custom_call" | custom-call | flops 3221225472 | bytes 6291456 | tf_op jit(solution)/shard_map/rotation_gradient/pallas_call | solution.py:476
  115.0 1.9 %results.1 = (f32[128,1024]{1,0:T(8,128)}, bf16[1,64,1024]{2,1,0:T(8,128)(2,1)}) custom-call(f32[128,1024]{1,0:T(8,128)} %get-tuple-element.4.total, bf16[1,64,1024]{2,1,0:T(8,128)(2,1)} %get-tuple-element.5.grad), custom_call_target="tpu_custom_call" | custom-call | tf_op jit(solution)/shard_map/results/pallas_call | solution.py:525
